TPU v7x, 32 devices: a whole 2x2x4 slice. The times are simulated.
32 devices in a mesh: ens: 2 (over y), lat: 16 (over z, x, core).
Axes of the slice: x: 2, y: 2, z: 4, core: 2. Of those that a mesh axis runs over, the one named last changes fastest.
Arguments:
- field: bfloat16 [2, 48, 96, 256], P('ens', 'lat'), parts along dimension 0, may hold values from -6 to 6
- filters: bfloat16 [2, 48, 256], replicated, may hold values from -5 to 5
- weight_in: bfloat16 [256, 512], replicated, may hold values from -0.375 to 0.375
- weight_out: bfloat16 [512, 256], replicated, may hold values from -0.25 to 0.25
- norm_gain: float32 [256], replicated, may hold values from 0.5 to 1.5
- cotangent: bfloat16 [2, 48, 96, 256], P('ens', 'lat'), parts along dimension 0, may hold values from -6 to 6
Outputs:
- block_out: bfloat16 [2, 48, 96, 256], P('ens', 'lat'), parts along dimension 0
- grad_field: bfloat16 [2, 48, 96, 256], P('ens', 'lat'), parts along dimension 0
- grad_filters: float32 [4, 48, 256], P('ens'), parts along dimension 0
- grad_weight_in: float32 [512, 512], P('ens'), parts along dimension 0
- grad_weight_out: float32 [1024, 256], P('ens'), parts along dimension 0
- grad_gain: float32 [512], P('ens'), parts along dimension 0
There are 2 independent parts, one for each index of `ens`. A program takes and returns all parts, laid end to end along the dimension named above; an argument that names none is the same for every part. Nothing has to cross between parts.
All inputs are finite; a program needn't handle non-finite values.
Results may differ from a plain program's by a relative error of at most 0.018.
Values may be sent and summed in bfloat16 or wider, within the bound.
A program may use at most 128 MiB of HBM per device.

v0:
```python
import math

import jax
import jax.numpy as jnp
from jax import lax
from jax.sharding import PartitionSpec as P

EPSILON = 1e-05


def compose_maps(earlier, later):
    e00, e01, e10, e11, ec0, ec1 = earlier
    l00, l01, l10, l11, lc0, lc1 = later
    return (
        l00 * e00 + l01 * e10,
        l00 * e01 + l01 * e11,
        l10 * e00 + l11 * e10,
        l10 * e01 + l11 * e11,
        l00 * ec0 + l01 * ec1 + lc0,
        l10 * ec0 + l11 * ec1 + lc1,
    )


def legendre(lat_total, orders, degree_count):
    colatitude = (jnp.arange(lat_total, dtype=jnp.float32) + 0.5) * (math.pi / lat_total)
    cosine = jnp.cos(colatitude)[None, :, None]
    sine_theta = jnp.sin(colatitude)[:, None]
    morder_row = orders.astype(jnp.float32)[None, :]
    log_start = 0.5 * (
        jnp.log((2.0 * morder_row + 1.0) / (4.0 * math.pi))
        + lax.lgamma(morder_row + 0.5)
        - lax.lgamma(morder_row + 1.0)
        - 0.5 * math.log(math.pi)
    ) + morder_row * jnp.log(sine_theta)
    diagonal = jnp.exp(log_start)[None, :, :]
    morder = orders.astype(jnp.float32)[None, None, :]
    order_rows = orders[None, None, :]
    degree = jnp.arange(degree_count, dtype=jnp.int32)[:, None, None]
    degree_f = degree.astype(jnp.float32)
    ratio_a = jnp.sqrt(
        (4.0 * degree_f * degree_f - 1.0) / jnp.maximum(degree_f * degree_f - morder * morder, 1.0)
    )
    previous_f = degree_f - 1.0
    ratio_b = jnp.sqrt(
        jnp.maximum(previous_f * previous_f - morder * morder, 0.0)
        / jnp.maximum(4.0 * previous_f * previous_f - 1.0, 1.0)
    )
    shape = (degree_count, lat_total, orders.shape[0])
    general = degree >= order_rows + 2
    step_one = degree == order_rows + 1
    at_start = degree == order_rows
    zero_map = jnp.zeros(shape, jnp.float32)
    first_row = jnp.where(
        general, ratio_a * cosine, jnp.where(step_one, jnp.sqrt(2.0 * morder + 3.0) * cosine, 0.0)
    )
    second_entry = jnp.where(general, -ratio_a * ratio_b, 0.0) + zero_map
    lower_entry = jnp.where(degree > order_rows, 1.0, 0.0) + zero_map
    offset = jnp.where(at_start, diagonal, 0.0)
    elements = (first_row, second_entry, lower_entry, zero_map, offset, zero_map)
    composed = lax.associative_scan(compose_maps, elements, axis=0)
    return jnp.transpose(composed[4], (1, 2, 0))


def latitude_weights(lat_total):
    colatitude = (jnp.arange(lat_total, dtype=jnp.float32) + 0.5) * (math.pi / lat_total)
    return jnp.sin(colatitude) * (math.pi / lat_total)


def forward_table(lon_cells, order_count):
    lon_index = jnp.arange(lon_cells, dtype=jnp.int32)[:, None]
    order_index = jnp.arange(order_count, dtype=jnp.int32)[None, :]
    angles = (lon_index * order_index % lon_cells).astype(jnp.float32) * (2.0 * math.pi / lon_cells)
    factor = 2.0 * math.pi / lon_cells
    return jnp.concatenate([jnp.cos(angles) * factor, -jnp.sin(angles) * factor], axis=1).astype(
        jnp.bfloat16
    )


def inverse_table(lon_cells, order_count):
    order_index = jnp.arange(order_count, dtype=jnp.int32)[:, None]
    lon_index = jnp.arange(lon_cells, dtype=jnp.int32)[None, :]
    angles = (lon_index * order_index % lon_cells).astype(jnp.float32) * (2.0 * math.pi / lon_cells)
    factor = jnp.where(order_index == 0, 1.0, 2.0)
    return jnp.concatenate([factor * jnp.cos(angles), -factor * jnp.sin(angles)], axis=0).astype(
        jnp.bfloat16
    )


def gelu_slope(preact):
    return (
        0.5 * (1.0 + lax.erf(preact * 0.7071067811865476))
        + preact * jnp.exp(-0.5 * preact * preact) * 0.3989422804014327
    )


def shards(field, filters, weight_in, weight_out, norm_gain, cotangent):
    lat_count = lax.axis_size("lat")
    position = lax.axis_index("lat")
    members, lat_rows, lon_cells, channels = field.shape
    degrees = lat_rows * lat_count
    orders = position * lat_rows + jnp.arange(lat_rows, dtype=jnp.int32)
    legendre_table = legendre(degrees, orders, degrees)
    synth_table = legendre_table.astype(jnp.bfloat16)
    analysis_table = (latitude_weights(degrees)[:, None, None] * legendre_table).astype(
        jnp.bfloat16
    )
    forward = forward_table(lon_cells, degrees)
    inverse = inverse_table(lon_cells, degrees)

    def to_orders(values):
        pieces = values.reshape(members, lat_rows, 2, lat_count, lat_rows, channels)
        arrived = lax.all_to_all(pieces, "lat", split_axis=3, concat_axis=1, tiled=True)
        return arrived.reshape(members, degrees, 2, lat_rows, channels)

    def to_grid(values):
        pieces = values.reshape(members, degrees, 2, 1, lat_rows, channels)
        arrived = lax.all_to_all(pieces, "lat", split_axis=1, concat_axis=3, tiled=True)
        return arrived.reshape(members, lat_rows, 2 * degrees, channels)

    def analyze(table, values):
        return jnp.einsum("jkl,bjrkc->brklc", table, values, preferred_element_type=jnp.float32)

    def synthesize(table, coeffs):
        return jnp.einsum("jkl,brklc->bjrkc", table, coeffs, preferred_element_type=jnp.float32)

    spectral = jnp.einsum(
        "bjkc,kn->bjnc", field, forward, preferred_element_type=jnp.float32
    ).astype(jnp.bfloat16)
    spectral_orders = to_orders(spectral)
    coeffs = analyze(analysis_table, spectral_orders).astype(jnp.bfloat16)
    coeffs_f32 = coeffs.astype(jnp.float32)
    spectral_gain = filters.astype(jnp.float32)
    real_part = coeffs_f32[:, 0] * spectral_gain[0] - coeffs_f32[:, 1] * spectral_gain[1]
    imag_part = coeffs_f32[:, 0] * spectral_gain[1] + coeffs_f32[:, 1] * spectral_gain[0]
    filtered = jnp.stack([real_part, imag_part], axis=1).astype(jnp.bfloat16)
    synthesized = synthesize(synth_table, filtered).astype(jnp.bfloat16)
    grid_side = to_grid(synthesized)
    back = jnp.einsum("bjnc,nk->bjkc", grid_side, inverse, preferred_element_type=jnp.float32)
    summed = (field.astype(jnp.float32) + back).astype(jnp.bfloat16)
    summed_f32 = summed.astype(jnp.float32)
    average = jnp.mean(summed_f32, axis=-1, keepdims=True)
    centered = summed_f32 - average
    inverse_std = lax.rsqrt(jnp.mean(centered * centered, axis=-1, keepdims=True) + EPSILON)
    normal = centered * inverse_std
    normed = (normal * norm_gain).astype(jnp.bfloat16)
    preact = jnp.einsum("bjkc,ch->bjkh", normed, weight_in, preferred_element_type=jnp.float32)
    hidden = jax.nn.gelu(preact, approximate=False).astype(jnp.bfloat16)
    block_out = (
        summed_f32
        + jnp.einsum("bjkh,hc->bjkc", hidden, weight_out, preferred_element_type=jnp.float32)
    ).astype(jnp.bfloat16)
    grad_pre = (
        jnp.einsum("bjkc,hc->bjkh", cotangent, weight_out, preferred_element_type=jnp.float32)
        * gelu_slope(preact)
    ).astype(jnp.bfloat16)
    grad_weight_in = jnp.einsum(
        "bjkc,bjkh->ch", normed, grad_pre, preferred_element_type=jnp.float32
    )
    grad_weight_out = jnp.einsum(
        "bjkh,bjkc->hc", hidden, cotangent, preferred_element_type=jnp.float32
    )
    grad_normed = jnp.einsum(
        "bjkh,ch->bjkc", grad_pre, weight_in, preferred_element_type=jnp.float32
    )
    grad_gain = jnp.sum(grad_normed * normal, axis=(0, 1, 2))
    grad_normal = grad_normed * norm_gain
    grad_summed = cotangent.astype(jnp.float32) + inverse_std * (
        grad_normal
        - jnp.mean(grad_normal, axis=-1, keepdims=True)
        - normal * jnp.mean(grad_normal * normal, axis=-1, keepdims=True)
    )
    grad_rounded = grad_summed.astype(jnp.bfloat16)
    grad_synth = jnp.einsum(
        "bjkc,nk->bjnc", grad_rounded, inverse, preferred_element_type=jnp.float32
    ).astype(jnp.bfloat16)
    grad_orders = to_orders(grad_synth)
    grad_filtered = analyze(synth_table, grad_orders)
    grad_real = grad_filtered[:, 0]
    grad_imag = grad_filtered[:, 1]
    filter_real = jnp.sum(coeffs_f32[:, 0] * grad_real + coeffs_f32[:, 1] * grad_imag, axis=(0, 1))
    filter_imag = jnp.sum(coeffs_f32[:, 0] * grad_imag - coeffs_f32[:, 1] * grad_real, axis=(0, 1))
    grad_filters = jnp.stack([filter_real, filter_imag], axis=0)
    coeff_real = grad_real * spectral_gain[0] + grad_imag * spectral_gain[1]
    coeff_imag = grad_imag * spectral_gain[0] - grad_real * spectral_gain[1]
    grad_coeffs = jnp.stack([coeff_real, coeff_imag], axis=1).astype(jnp.bfloat16)
    grad_spectral = synthesize(analysis_table, grad_coeffs).astype(jnp.bfloat16)
    grad_grid = to_grid(grad_spectral)
    grad_field = (
        grad_summed
        + jnp.einsum("bjnc,kn->bjkc", grad_grid, forward, preferred_element_type=jnp.float32)
    ).astype(jnp.bfloat16)
    grad_filters, grad_weight_in, grad_weight_out, grad_gain = lax.psum(
        (grad_filters, grad_weight_in, grad_weight_out, grad_gain), "lat"
    )
    grad_scale = 1.0 / math.sqrt(members * degrees * lon_cells)
    return (
        block_out,
        grad_field,
        grad_filters * grad_scale,
        grad_weight_in * grad_scale,
        grad_weight_out * grad_scale,
        grad_gain * grad_scale,
    )


def solution(mesh):
    placed = (P("ens", "lat", None, None), P(), P(), P(), P(), P("ens", "lat", None, None))
    return jax.shard_map(
        shards,
        mesh=mesh,
        in_specs=placed,
        out_specs=(
            P("ens", "lat", None, None),
            P("ens", "lat", None, None),
            P("ens", None, None),
            P("ens", None),
            P("ens", None),
            P("ens"),
        ),
        check_vma=False,
    )
```

profile of v0, /device:TPU:0, one launch (start us, length us, event | category | flops | bytes accessed | tf_op | source)
XLA Modules:
  0.0 201.6 jit_solution(5559005247429837679)
XLA Ops:
  7.3 1.1 fusion.8
  8.5 0.8 copy.110
  9.3 7.4 %all-to-all-start = ((bf16[1,3,2,16,3,256]{5,2,4,1,0,3:T(2,128)(2,1)}), bf16[1,3,2,16,3,256]{5,2,4,1,0,3:T(2,128)(2,1)S(1)}, u32[]{:S(2)}, u32[]{:S(2)}) async-start(bf16[1,3,2,16,3,256]{5,2,4,1,0,3:T(2,128)(2,1)} %copy.110), calls=%async_computation | async-start | bytes 294912 | tf_op jit(solution)/shard_map/all_to_all | solution.py:112
  20.9 0.7 copy-done.5
  22.0 2.9 %all-to-all-done = bf16[1,3,2,16,3,256]{5,2,4,1,0,3:T(2,128)(2,1)S(1)} async-done(((bf16[1,3,2,16,3,256]{5,2,4,1,0,3:T(2,128)(2,1)}), bf16[1,3,2,16,3,256]{5,2,4,1,0,3:T(2,128)(2,1)S(1)}, u32[]{:S(2)}, u32[]{:S(2)}) %all-to-all-start) | async-done | bytes 147488 | tf_op jit(solution)/shard_map/all_to_all | solution.py:112
  25.4 0.8 copy.117
  26.1 3.5 %all-to-all-start.1 = ((bf16[1,48,2,1,3,256]{5,2,4,3,0,1:T(2,128)(2,1)}), bf16[1,48,2,1,3,256]{5,2,4,3,0,1:T(2,128)(2,1)S(1)}, u32[]{:S(2)}, u32[]{:S(2)}) async-start(bf16[1,48,2,1,3,256]{5,2,4,3,0,1:T(2,128)(2,1)} %copy.117), calls=%async_computation.1 | async-start | bytes 294912 | tf_op jit(solution)/shard_map/all_to_all | solution.py:117
  29.8 8.0 %all-to-all-done.1 = bf16[1,48,2,1,3,256]{5,2,4,3,0,1:T(2,128)(2,1)S(1)} async-done(((bf16[1,48,2,1,3,256]{5,2,4,3,0,1:T(2,128)(2,1)}), bf16[1,48,2,1,3,256]{5,2,4,3,0,1:T(2,128)(2,1)S(1)}, u32[]{:S(2)}, u32[]{:S(2)}) %all-to-all-start.1) | async-done | bytes 147488 | tf_op jit(solution)/shard_map/all_to_all | solution.py:117
  38.0 0.8 copy-done.2
  39.4 0.7 copy-done.6
  40.1 0.4 fusion.57
  40.5 0.5 copy-done.1
  41.5 0.4 fusion.28
  41.8 30.3 %psum.31 = f32[256]{0:T(256)S(1)} all-reduce(f32[256]{0:T(256)S(1)} %get-tuple-element.6), channel_id=1, replica_groups=mesh['ens'=2,'lat'=16] {'lat'}, use_global_device_ids=true, to_apply=%region_10.11 | all-reduce | flops 256 | bytes 2048 | tf_op jit(solution)/shard_map/psum | solution.py:192
  72.2 0.4 fusion.10
  72.7 0.8 copy.120
  73.6 3.5 %all-to-all-start.2 = ((bf16[1,3,2,16,3,256]{5,2,4,1,0,3:T(2,128)(2,1)}), bf16[1,3,2,16,3,256]{5,2,4,1,0,3:T(2,128)(2,1)S(1)}, u32[]{:S(2)}, u32[]{:S(2)}) async-start(bf16[1,3,2,16,3,256]{5,2,4,1,0,3:T(2,128)(2,1)} %copy.120), calls=%async_computation.2 | async-start | bytes 294912 | tf_op jit(solution)/shard_map/all_to_all | solution.py:112
  77.1 1.3 fusion.17
  78.4 1.1 convolution_bitcast_fusion
  79.5 1.3 convolution_bitcast_fusion.1
  80.8 4.4 %all-to-all-done.2 = bf16[1,3,2,16,3,256]{5,2,4,1,0,3:T(2,128)(2,1)S(1)} async-done(((bf16[1,3,2,16,3,256]{5,2,4,1,0,3:T(2,128)(2,1)}), bf16[1,3,2,16,3,256]{5,2,4,1,0,3:T(2,128)(2,1)S(1)}, u32[]{:S(2)}, u32[]{:S(2)}) %all-to-all-start.2) | async-done | bytes 147488 | tf_op jit(solution)/shard_map/all_to_all | solution.py:112
  85.8 0.8 copy.129
  86.5 3.5 %all-to-all-start.3 = ((bf16[1,48,2,1,3,256]{5,2,4,3,0,1:T(2,128)(2,1)}), bf16[1,48,2,1,3,256]{5,2,4,3,0,1:T(2,128)(2,1)S(1)}, u32[]{:S(2)}, u32[]{:S(2)}) async-start(bf16[1,48,2,1,3,256]{5,2,4,3,0,1:T(2,128)(2,1)} %copy.129), calls=%async_computation.3 | async-start | bytes 294912 | tf_op jit(solution)/shard_map/all_to_all | solution.py:117
  90.1 0.6 pad_maximum_fusion.2
  90.8 0.6 broadcast_multiply_fusion.10
  91.4 0.9 fusion.4
  92.3 6.0 %all-to-all-done.3 = bf16[1,48,2,1,3,256]{5,2,4,3,0,1:T(2,128)(2,1)S(1)} async-done(((bf16[1,48,2,1,3,256]{5,2,4,3,0,1:T(2,128)(2,1)}), bf16[1,48,2,1,3,256]{5,2,4,3,0,1:T(2,128)(2,1)S(1)}, u32[]{:S(2)}, u32[]{:S(2)}) %all-to-all-start.3) | async-done | bytes 147488 | tf_op jit(solution)/shard_map/all_to_all | solution.py:117
  98.4 0.9 fusion.5
  99.4 91.1 %all-reduce.21.cloned.1.call-done = (f32[2,48,256]{2,1,0:T(8,128)}, f32[256,512]{1,0:T(8,128)}, f32[512,256]{1,0:T(8,128)}) async-done(((f32[2,48,256]{2,1,0:T(8,128)}, f32[256,512]{1,0:T(8,128)}, f32[512,256]{1,0:T(8,128)}), (f32[2,48,256]{2,1,0:T(8,128)}, f32[256,512]{1,0:T(8,128)}, f32[512,256]{1,0:T(8,128)})) %all-reduce.21.cloned.1.call-update) | async-done | bytes 1146896 | tf_op jit(solution)/shard_map/psum | solution.py:192
  190.4 1.5 broadcast_multiply_fusion.2
  192.0 1.9 broadcast_multiply_fusion.1
  193.9 0.8 broadcast_multiply_fusion
  (175 shorter events, 7.1 us)
Async XLA Ops:
  7.2 32.2 %copy-start = (bf16[256,512]{1,0:T(8,128)(2,1)S(1)}, bf16[256,512]{1,0:T(8,128)(2,1)}, u32[]{:S(2)}) copy-start(bf16[256,512]{1,0:T(8,128)(2,1)} %param.8) | copy-start | bytes 786436
  9.3 15.6 %all-to-all-start = ((bf16[1,3,2,16,3,256]{5,2,4,1,0,3:T(2,128)(2,1)}), bf16[1,3,2,16,3,256]{5,2,4,1,0,3:T(2,128)(2,1)S(1)}, u32[]{:S(2)}, u32[]{:S(2)}) async-start(bf16[1,3,2,16,3,256]{5,2,4,1,0,3:T(2,128)(2,1)} %copy.110), calls=%async_computation | async-start | bytes 294912 | tf_op jit(solution)/shard_map/all_to_all | solution.py:112
  20.9 0.8 copy-start.5
  26.1 11.7 %all-to-all-start.1 = ((bf16[1,48,2,1,3,256]{5,2,4,3,0,1:T(2,128)(2,1)}), bf16[1,48,2,1,3,256]{5,2,4,3,0,1:T(2,128)(2,1)S(1)}, u32[]{:S(2)}, u32[]{:S(2)}) async-start(bf16[1,48,2,1,3,256]{5,2,4,3,0,1:T(2,128)(2,1)} %copy.117), calls=%async_computation.1 | async-start | bytes 294912 | tf_op jit(solution)/shard_map/all_to_all | solution.py:117
  37.9 0.9 copy-start.2
  39.4 0.7 copy-start.6
  40.1 0.9 copy-start.1
  40.1 1.0 copy-start.4
  73.6 11.7 %all-to-all-start.2 = ((bf16[1,3,2,16,3,256]{5,2,4,1,0,3:T(2,128)(2,1)}), bf16[1,3,2,16,3,256]{5,2,4,1,0,3:T(2,128)(2,1)S(1)}, u32[]{:S(2)}, u32[]{:S(2)}) async-start(bf16[1,3,2,16,3,256]{5,2,4,1,0,3:T(2,128)(2,1)} %copy.120), calls=%async_computation.2 | async-start | bytes 294912 | tf_op jit(solution)/shard_map/all_to_all | solution.py:112
  86.5 11.7 %all-to-all-start.3 = ((bf16[1,48,2,1,3,256]{5,2,4,3,0,1:T(2,128)(2,1)}), bf16[1,48,2,1,3,256]{5,2,4,3,0,1:T(2,128)(2,1)S(1)}, u32[]{:S(2)}, u32[]{:S(2)}) async-start(bf16[1,48,2,1,3,256]{5,2,4,3,0,1:T(2,128)(2,1)} %copy.129), calls=%async_computation.3 | async-start | bytes 294912 | tf_op jit(solution)/shard_map/all_to_all | solution.py:117
  90.1 100.4 %all-reduce.21.cloned.1.call-start = ((), (), s32[]{:S(2)}) async-start(), calls=%async_computation.4 | async-start | bytes 2293760 | tf_op jit(solution)/shard_map/psum | solution.py:192
  192.0 1.9 copy-start.3
Sparse Core Ops, SparseCore 0:
  95.2 95.1 all-reduce.20
where the time goes:
time: 202 us
  waiting for transfers between devices  112 us (55%)
  blocking collectives  30.3 us (15%)
  starting transfers between devices  17.9 us (9%)
  between operations  14.7 us (7%)
  other arithmetic  9.31 us (5%)
  local copies, waits for them, and re-layouts  8.97 us (4%)
  matrix products  7.95 us (4%)
    psum x1, waiting for transfers between devices, shards(): lax.psum((grad_filters, grad_weight_in, grad_weight_out, grad_gain), 'lat')  91.1 us
    psum x1, blocking collectives, shards(): lax.psum((grad_filters, grad_weight_in, grad_weight_out, grad_gain), 'lat')  30.3 us
    all_to_all x2, waiting for transfers between devices, to_grid(): lax.all_to_all(pieces, 'lat', split_axis=1, concat_axis=3, tiled=True)  14 us
    all_to_all x2, starting transfers between devices, to_orders(): lax.all_to_all(pieces, 'lat', split_axis=3, concat_axis=1, tiled=True)  10.9 us
    all_to_all x2, waiting for transfers between devices, to_orders(): lax.all_to_all(pieces, 'lat', split_axis=3, concat_axis=1, tiled=True)  7.36 us
    all_to_all x2, starting transfers between devices, to_grid(): lax.all_to_all(pieces, 'lat', split_axis=1, concat_axis=3, tiled=True)  7.03 us
  transfers between devices with their start and end apart: 5, of which 5 were waited for; matrix products, arithmetic and copies ran while one was open for 6% of the time, Pallas kernels for 0%

commit v1 on v0

--- a/solution.py
+++ b/solution.py
@@ -1,8 +1,13 @@
+import functools
 import math
 
 import jax
 import jax.numpy as jnp
+import ml_dtypes
+import numpy as np
 from jax import lax
+from jax.experimental import pallas as pl
+from jax.experimental.pallas import tpu as pltpu
 from jax.sharding import PartitionSpec as P
 
 EPSILON = 1e-05
@@ -203,10 +208,494 @@
     )
 
 
+HALF = 128
+SLOT = 8
+TILE = 16
+MESH = pl.DeviceIdType.MESH
+
+
+def dot(a, b):
+    return jnp.dot(a, b, preferred_element_type=jnp.float32)
+
+
+def dot_nt(a, b):
+    return lax.dot_general(a, b, (((1,), (1,)), ((), ())), preferred_element_type=jnp.float32)
+
+
+def dot_tn(a, b):
+    return lax.dot_general(a, b, (((0,), (0,)), ((), ())), preferred_element_type=jnp.float32)
+
+
+def fused_kernel(
+    n, rows, lon, scale,
+    field, filters, w_in, w_out, gain, cot, fwd_nk, inv_kn, inv_nk, fwd_kn, tables,
+    block_out, grad_field, grad_filters, grad_w_in, grad_w_out, grad_gain,
+    send, recv, fsend, frecv, fgather, wsend, wpair, wchips, wrecv, wgather,
+    table, up, summed, normed, hidden, grad_pre, grad_sum, coeffs,
+    x0, x1, y0, y1, f0, f1, nat,
+    send_sem, recv_sem, chip_send, chip_recv, pair_send, pair_recv, table_sem,
+):
+    me = lax.axis_index("lat")
+    ens = lax.axis_index("ens")
+    core = lax.rem(me, 2)
+    chip = me // 2
+    chips = n // 2
+    partner = me + 1 - 2 * core
+    degrees = n * rows
+    bf16 = jnp.bfloat16
+
+    barrier = pltpu.get_barrier_semaphore()
+
+    def greet(k, _):
+        pl.semaphore_signal(
+            barrier, inc=1, device_id=(ens, lax.rem(me + k, n)), device_id_type=MESH
+        )
+        return 0
+
+    lax.fori_loop(1, n, greet, 0)
+    fetch = pltpu.make_async_copy(tables.at[me], table, table_sem)
+    fetch.start()
+
+    def exchange(phase, source, target):
+        def copy(k):
+            to = lax.rem(me + k, n)
+            return pltpu.make_async_remote_copy(
+                src_ref=source(to), dst_ref=target(me),
+                send_sem=send_sem.at[phase, k], recv_sem=recv_sem.at[phase, k],
+                device_id=(ens, to), device_id_type=MESH,
+            )
+
+        def landing(k):
+            origin = lax.rem(me + n - k, n)
+            return pltpu.make_async_remote_copy(
+                src_ref=source(origin), dst_ref=target(origin),
+                send_sem=send_sem.at[phase, k], recv_sem=recv_sem.at[phase, k],
+                device_id=(ens, origin), device_id_type=MESH,
+            )
+
+        def start(k, _):
+            copy(k).start()
+            return 0
+
+        def arrive(k, _):
+            landing(k).wait_recv()
+            return 0
+
+        def leave(k, _):
+            copy(k).wait_send()
+            return 0
+
+        return (
+            lambda: lax.fori_loop(1, n, start, 0),
+            lambda: lax.fori_loop(1, n, arrive, 0),
+            lambda: lax.fori_loop(1, n, leave, 0),
+        )
+
+    def all_to_all(phase):
+        return exchange(phase, lambda i: send.at[phase, i], lambda i: recv.at[phase, i])
+
+    def pack_grid(phase, parts):
+        pieces = [p[:, h : h + HALF].reshape(n, SLOT, HALF) for h in (0, HALF) for p in parts]
+        send[phase] = jnp.concatenate(pieces, axis=1).astype(bf16)
+        recv[phase, me] = send[phase, me]
+
+    def pack_orders(phase):
+        y = [v[...].reshape(n, rows * SLOT, HALF) for v in (y0, y1)]
+        send[phase] = jnp.concatenate(y, axis=1).astype(bf16)
+        recv[phase, me] = send[phase, me]
+
+    def unpack_orders(phase):
+        arrived = recv[phase].astype(jnp.float32)
+        x0[...] = arrived[:, : rows * SLOT].reshape(degrees * SLOT, HALF)
+        x1[...] = arrived[:, rows * SLOT :].reshape(degrees * SLOT, HALF)
+
+    def unpack_grid(phase, j):
+        parts = [
+            recv[phase, :, pl.ds(0, 2 * rows * SLOT), :].astype(jnp.float32)[
+                :, (h * rows + j) * SLOT : (h * rows + j + 1) * SLOT
+            ].reshape(n * SLOT, HALF)
+            for h in (0, 1)
+        ]
+        return jnp.concatenate(parts, axis=1).astype(bf16)
+
+    def of_order(m):
+        picked = [
+            v[pl.ds(r * rows + m, degrees, stride=SLOT), :] for r in (0, 1) for v in (x0, x1)
+        ]
+        return jnp.concatenate(picked, axis=1).astype(bf16)
+
+    def to_order(m, value):
+        for r in (0, 1):
+            for h, v in enumerate((y0, y1)):
+                at = (2 * r + h) * HALF
+                v[pl.ds(r * rows + m, degrees, stride=SLOT), :] = value[:, at : at + HALF]
+
+    start0, arrive0, leave0 = all_to_all(0)
+    pack_grid(0, [dot(fwd_nk[...], field[pl.ds(j * lon, lon), :]) for j in range(rows)])
+    pl.semaphore_wait(barrier, n - 1)
+    start0()
+    y0[...] = jnp.zeros_like(y0)
+    y1[...] = jnp.zeros_like(y1)
+    f0[...] = jnp.zeros_like(f0)
+    f1[...] = jnp.zeros_like(f1)
+    for j in range(rows):
+        at = pl.ds(j * lon, lon)
+        up[at, :] = dot_nt(cot[at, :], w_out[...])
+    fetch.wait()
+    g0 = filters[0].astype(jnp.float32)
+    g1 = filters[1].astype(jnp.float32)
+    wide = 2 * HALF
+    arrive0()
+
+    start1, arrive1, leave1 = all_to_all(1)
+    unpack_orders(0)
+    for m in range(rows):
+        c = dot(table[0, m], of_order(m)).astype(bf16)
+        coeffs[m] = c
+        c = c.astype(jnp.float32)
+        cr, ci = c[:, :wide], c[:, wide:]
+        filtered = jnp.concatenate([cr * g0 - ci * g1, cr * g1 + ci * g0], axis=1).astype(bf16)
+        to_order(m, dot(table[1, m], filtered))
+    pack_orders(1)
+    start1()
+    arrive1()
+
+    start2, arrive2, leave2 = all_to_all(2)
+    gain_row = gain[...]
+    gain_sum = jnp.zeros_like(gain_row)
+    parts = []
+    for j in range(rows):
+        at = pl.ds(j * lon, lon)
+        back = dot(inv_kn[...], unpack_grid(1, j))
+        s = (field[at, :].astype(jnp.float32) + back).astype(bf16)
+        summed[at, :] = s
+        s = s.astype(jnp.float32)
+        centered = s - jnp.mean(s, axis=-1, keepdims=True)
+        inverse_std = lax.rsqrt(jnp.mean(centered * centered, axis=-1, keepdims=True) + EPSILON)
+        normal = centered * inverse_std
+        nb = (normal * gain_row).astype(bf16)
+        normed[at, :] = nb
+        pre = dot(nb, w_in[...])
+        phi = 0.5 * (1.0 + lax.erf(pre * 0.7071067811865476))
+        hidden[at, :] = (pre * phi).astype(bf16)
+        slope = phi + pre * jnp.exp(-0.5 * pre * pre) * 0.3989422804014327
+        gp = (up[at, :] * slope).astype(bf16)
+        grad_pre[at, :] = gp
+        gn = dot_nt(gp, w_in[...])
+        gain_sum = gain_sum + jnp.sum(gn * normal, axis=0, keepdims=True)
+        v = gn * gain_row
+        gs = cot[at, :].astype(jnp.float32) + inverse_std * (
+            v
+            - jnp.mean(v, axis=-1, keepdims=True)
+            - normal * jnp.mean(v * normal, axis=-1, keepdims=True)
+        )
+        grad_sum[at, :] = gs
+        parts.append(dot(inv_nk[...], gs.astype(bf16)))
+    pack_grid(2, parts)
+    start2()
+
+    mid = w_in.shape[0] // n
+    gi = dot_tn(normed[...], grad_pre[...]).astype(bf16)
+    wsend[:, :, :mid, :] = gi.reshape(2, chips, mid, gi.shape[1])
+    go = dot_tn(hidden[...], cot[...]).astype(bf16).reshape(2, chips, 2 * mid, w_out.shape[1])
+    wsend[:, :, mid:, :] = jnp.concatenate([go[:, :, :mid], go[:, :, mid:]], axis=3)
+
+    def pair_copy(slot, source, target):
+        return pltpu.make_async_remote_copy(
+            src_ref=source, dst_ref=target,
+            send_sem=pair_send.at[slot], recv_sem=pair_recv.at[slot],
+            device_id=(ens, partner), device_id_type=MESH,
+        )
+
+    def chip_exchange(phase, source, target):
+        def copy(k):
+            to = lax.rem(chip + k, chips)
+            return pltpu.make_async_remote_copy(
+                src_ref=source(to), dst_ref=target(chip),
+                send_sem=chip_send.at[phase, k], recv_sem=chip_recv.at[phase, k],
+                device_id=(ens, 2 * to + core), device_id_type=MESH,
+            )
+
+        def landing(k):
+            origin = lax.rem(chip + chips - k, chips)
+            return pltpu.make_async_remote_copy(
+                src_ref=source(origin), dst_ref=target(origin),
+                send_sem=chip_send.at[phase, k], recv_sem=chip_recv.at[phase, k],
+                device_id=(ens, 2 * origin + core), device_id_type=MESH,
+            )
+
+        def start(k, _):
+            copy(k).start()
+            return 0
+
+        def arrive(k, _):
+            landing(k).wait_recv()
+            return 0
+
+        def leave(k, _):
+            copy(k).wait_send()
+            return 0
+
+        return (
+            lambda: lax.fori_loop(1, chips, start, 0),
+            lambda: lax.fori_loop(1, chips, arrive, 0),
+            lambda: lax.fori_loop(1, chips, leave, 0),
+        )
+
+    pair0 = pair_copy(0, wsend.at[1 - core], wpair)
+    pair0.start()
+    for j in range(rows):
+        at = pl.ds(j * lon, lon)
+        block_out[at, :] = (
+            summed[at, :].astype(jnp.float32) + dot(hidden[at, :], w_out[...])
+        ).astype(bf16)
+    pair0.wait_recv()
+    scatter_start, scatter_arrive, scatter_leave = chip_exchange(
+        0, lambda i: wchips.at[i], lambda i: wrecv.at[i]
+    )
+    wchips[...] = (wsend[core].astype(jnp.float32) + wpair[...].astype(jnp.float32)).astype(bf16)
+    wrecv[chip] = wchips[chip]
+    scatter_start()
+
+    arrive2()
+    start3, arrive3, leave3 = all_to_all(3)
+    unpack_orders(2)
+    fr = jnp.zeros((degrees, wide), jnp.float32)
+    fi = jnp.zeros((degrees, wide), jnp.float32)
+    for m in range(rows):
+        g = dot(table[2, m], of_order(m))
+        gr, gi = g[:, :wide], g[:, wide:]
+        c = coeffs[m].astype(jnp.float32)
+        cr, ci = c[:, :wide], c[:, wide:]
+        fr = fr + (cr * gr + ci * gi)
+        fi = fi + (cr * gi - ci * gr)
+        gc = jnp.concatenate([gr * g0 + gi * g1, gi * g0 - gr * g1], axis=1).astype(bf16)
+        to_order(m, dot(table[3, m], gc))
+    pack_orders(3)
+    start3()
+
+    for r, f in enumerate((fr, fi)):
+        for h in (0, 1):
+            nat[2 * r + h] = f[:, h * HALF : (h + 1) * HALF]
+    for h, f in enumerate((f0, f1)):
+        for r in (0, 1):
+            for m in range(rows):
+                f[pl.ds(r * rows + m, n, stride=SLOT), :] = nat[
+                    2 * r + h, pl.ds(m, n, stride=rows), :
+                ]
+        f[pl.ds(2 * rows, n, stride=SLOT), :] = jnp.broadcast_to(
+            gain_sum[:, h * HALF : (h + 1) * HALF], (n, HALF)
+        )
+    fsend[...] = jnp.concatenate(
+        [f[...].reshape(n, SLOT, HALF) for f in (f0, f1)], axis=1
+    ).astype(bf16)
+    frecv[me] = fsend[me]
+    start4, arrive4, leave4 = exchange(4, lambda i: fsend.at[i], lambda i: frecv.at[i])
+    start4()
+
+    gather_start, gather_arrive, gather_leave = chip_exchange(
+        1, lambda i: wgather.at[core, chip], lambda i: wgather.at[core, i]
+    )
+    scatter_arrive()
+    wgather[core, chip] = jnp.sum(wrecv[...].astype(jnp.float32), axis=0).astype(bf16)
+    gather_start()
+
+    arrive4()
+    ftotal = jnp.sum(frecv[...].astype(jnp.float32), axis=0)
+    grad_gain[...] = scale * jnp.concatenate(
+        [ftotal[2 * rows : 2 * rows + 1], ftotal[SLOT + 2 * rows : SLOT + 2 * rows + 1]], axis=1
+    )
+    fgather[me] = ftotal.astype(bf16)
+    start5, arrive5, leave5 = exchange(5, lambda i: fgather.at[me], lambda i: fgather.at[i])
+    start5()
+
+    arrive3()
+    for j in range(rows):
+        at = pl.ds(j * lon, lon)
+        grad_field[at, :] = (grad_sum[at, :] + dot(fwd_kn[...], unpack_grid(3, j))).astype(bf16)
+
+    gather_arrive()
+    pair1 = pair_copy(1, wgather.at[core], wgather.at[core])
+    pair1_in = pair_copy(1, wgather.at[1 - core], wgather.at[1 - core])
+    pair1.start()
+
+    arrive5()
+    fall = fgather[...].astype(jnp.float32) * scale
+    f0[...] = fall[:, :SLOT].reshape(n * SLOT, HALF)
+    f1[...] = fall[:, SLOT:].reshape(n * SLOT, HALF)
+    for h, f in enumerate((f0, f1)):
+        for r in (0, 1):
+            for m in range(rows):
+                nat[2 * r + h, pl.ds(m, n, stride=rows), :] = f[
+                    pl.ds(r * rows + m, n, stride=SLOT), :
+                ]
+            grad_filters[r, :, h * HALF : (h + 1) * HALF] = nat[2 * r + h]
+
+    pair1_in.wait_recv()
+    full = w_in.shape[1]
+    for c in (0, 1):
+        grad_w_in[pl.ds(c * chips * mid, chips * mid), :] = (
+            wgather[c, :, :mid, :].astype(jnp.float32) * scale
+        ).reshape(chips * mid, full)
+        both = wgather[c, :, mid:, :].astype(jnp.float32) * scale
+        grad_w_out[pl.ds(2 * c * chips * mid, 2 * chips * mid), :] = jnp.concatenate(
+            [both[:, :, : full // 2], both[:, :, full // 2 :]], axis=1
+        ).reshape(2 * chips * mid, full // 2)
+
+    for leave in (leave0, leave1, leave2, leave3, leave4, leave5, scatter_leave, gather_leave):
+        leave()
+    pair0.wait_send()
+    pair1.wait_send()
+
+
+def legendre_constants(total):
+    theta = (np.arange(total) + 0.5) * (math.pi / total)
+    x, sine = np.cos(theta), np.sin(theta)
+    p = np.zeros((total, total, total), np.float64)
+    for m in range(total):
+        log_start = 0.5 * (
+            math.log((2.0 * m + 1.0) / (4.0 * math.pi))
+            + math.lgamma(m + 0.5)
+            - math.lgamma(m + 1.0)
+            - 0.5 * math.log(math.pi)
+        )
+        p[:, m, m] = np.exp(log_start + m * np.log(sine))
+        if m + 1 < total:
+            p[:, m, m + 1] = math.sqrt(2.0 * m + 3.0) * x * p[:, m, m]
+        for l in range(m + 2, total):
+            a = math.sqrt((4.0 * l * l - 1.0) / (l * l - m * m))
+            b = math.sqrt(((l - 1.0) ** 2 - m * m) / (4.0 * (l - 1.0) ** 2 - 1.0))
+            p[:, m, l] = a * (x * p[:, m, l - 1] - b * p[:, m, l - 2])
+    weights = sine * (math.pi / total)
+    return p, weights[:, None, None] * p
+
+
+def slot_rows(table, n, rows):
+    lon = table.shape[2]
+    spread = np.zeros((n, SLOT, lon), np.float64)
+    spread[:, : 2 * rows] = (
+        table.reshape(2, n, rows, lon).transpose(1, 0, 2, 3).reshape(n, 2 * rows, lon)
+    )
+    return spread.reshape(n * SLOT, lon)
+
+
+def fused_constants(n, rows, lon):
+    total = n * rows
+    synth, analysis = legendre_constants(total)
+    by_owner = lambda t, axes: t.transpose(axes).reshape(n, rows, total, total)
+    tables = np.stack(
+        [
+            by_owner(analysis, (1, 2, 0)),
+            by_owner(synth, (1, 0, 2)),
+            by_owner(synth, (1, 2, 0)),
+            by_owner(analysis, (1, 0, 2)),
+        ],
+        axis=1,
+    )
+    angle = (np.arange(total)[:, None] * np.arange(lon)[None, :] % lon) * (2.0 * math.pi / lon)
+    wave = np.stack([np.cos(angle), -np.sin(angle)])
+    forward = slot_rows(wave * (2.0 * math.pi / lon), n, rows)
+    inverse = slot_rows(wave * np.where(np.arange(total) == 0, 1.0, 2.0)[:, None], n, rows)
+    cast = lambda t: np.asarray(t, np.float32).astype(ml_dtypes.bfloat16)
+    return (
+        cast(forward), cast(inverse.T), cast(inverse), cast(forward.T), cast(tables),
+    )
+
+
+def fused(field, filters, weight_in, weight_out, norm_gain, cotangent):
+    n = lax.axis_size("lat")
+    _, rows, lon, channels = field.shape
+    hid = weight_in.shape[1]
+    cells, total, chips = rows * lon, rows * n, n // 2
+    mid = channels // n
+    f32, bf16 = jnp.float32, jnp.bfloat16
+    scale = 1.0 / math.sqrt(total * lon)
+    constants = fused_constants(n, rows, lon)
+    vmem = pl.BlockSpec(memory_space=pltpu.VMEM)
+    phases = 4
+    outs = pl.pallas_call(
+        functools.partial(fused_kernel, n, rows, lon, scale),
+        out_shape=(
+            jax.ShapeDtypeStruct((cells, channels), bf16),
+            jax.ShapeDtypeStruct((cells, channels), bf16),
+            jax.ShapeDtypeStruct((2, total, channels), f32),
+            jax.ShapeDtypeStruct((channels, hid), f32),
+            jax.ShapeDtypeStruct((hid, channels), f32),
+            jax.ShapeDtypeStruct((1, channels), f32),
+        ),
+        in_specs=[vmem] * 10 + [pl.BlockSpec(memory_space=pl.ANY)],
+        out_specs=(vmem,) * 6,
+        scratch_shapes=[
+            pltpu.VMEM((phases, n, 2 * rows * SLOT, HALF), bf16),
+            pltpu.VMEM((phases, n, 2 * rows * SLOT, HALF), bf16),
+            pltpu.VMEM((n, 2 * SLOT, HALF), bf16),
+            pltpu.VMEM((n, 2 * SLOT, HALF), bf16),
+            pltpu.VMEM((n, 2 * SLOT, HALF), bf16),
+            pltpu.VMEM((2, chips, 2 * mid, hid), bf16),
+            pltpu.VMEM((chips, 2 * mid, hid), bf16),
+            pltpu.VMEM((chips, 2 * mid, hid), bf16),
+            pltpu.VMEM((chips, 2 * mid, hid), bf16),
+            pltpu.VMEM((2, chips, 2 * mid, hid), bf16),
+            pltpu.VMEM((4, rows, total, total), bf16),
+            pltpu.VMEM((cells, hid), f32),
+            pltpu.VMEM((cells, channels), bf16),
+            pltpu.VMEM((cells, channels), bf16),
+            pltpu.VMEM((cells, hid), bf16),
+            pltpu.VMEM((cells, hid), bf16),
+            pltpu.VMEM((cells, channels), f32),
+            pltpu.VMEM((rows, total, 2 * channels), bf16),
+            pltpu.VMEM((total * SLOT, HALF), f32),
+            pltpu.VMEM((total * SLOT, HALF), f32),
+            pltpu.VMEM((total * SLOT, HALF), f32),
+            pltpu.VMEM((total * SLOT, HALF), f32),
+            pltpu.VMEM((n * SLOT, HALF), f32),
+            pltpu.VMEM((n * SLOT, HALF), f32),
+            pltpu.VMEM((4, total, HALF), f32),
+            pltpu.SemaphoreType.DMA((6, n)),
+            pltpu.SemaphoreType.DMA((6, n)),
+            pltpu.SemaphoreType.DMA((2, chips)),
+            pltpu.SemaphoreType.DMA((2, chips)),
+            pltpu.SemaphoreType.DMA((2,)),
+            pltpu.SemaphoreType.DMA((2,)),
+            pltpu.SemaphoreType.DMA,
+        ],
+        compiler_params=pltpu.CompilerParams(
+            collective_id=0, has_side_effects=True, vmem_limit_bytes=40 * 1024 * 1024
+        ),
+    )(
+        field.reshape(cells, channels), filters, weight_in, weight_out,
+        norm_gain.reshape(1, channels), cotangent.reshape(cells, channels),
+        *[jnp.asarray(t) for t in constants],
+    )
+    return (
+        outs[0].reshape(field.shape), outs[1].reshape(field.shape),
+        outs[2], outs[3], outs[4], outs[5].reshape(channels),
+    )
+
+
+def block(field, filters, weight_in, weight_out, norm_gain, cotangent):
+    n = lax.axis_size("lat")
+    members, rows, lon, channels = field.shape
+    hid = weight_in.shape[1]
+    fits = (
+        members == 1
+        and n % 2 == 0
+        and 2 * rows < SLOT
+        and channels == 2 * HALF
+        and hid == 2 * channels
+        and channels % (TILE * n) == 0
+        and (rows * n) % TILE == 0
+        and lon % TILE == 0
+        and rows * lon * hid <= 512 * 1024
+    )
+    chosen = fused if fits else shards
+    return chosen(field, filters, weight_in, weight_out, norm_gain, cotangent)
+
+
 def solution(mesh):
     placed = (P("ens", "lat", None, None), P(), P(), P(), P(), P("ens", "lat", None, None))
     return jax.shard_map(
-        shards,
+        block,
         mesh=mesh,
         in_specs=placed,
         out_specs=(

time: 202 us -> 64.2 us (0.32)
  waiting for transfers between devices: 112 us -> 0 us
  Pallas kernels: 0 us -> 49 us
  blocking collectives: 30.3 us -> 0 us
  starting transfers between devices: 17.9 us -> 0 us
  between operations: 14.7 us -> 0.66 us
  other arithmetic: 9.31 us -> 0 us
  matrix products: 7.95 us -> 0 us
  local copies, waits for them, and re-layouts: 8.97 us -> 14 us
    psum x1 -> x0, waiting for transfers between devices: 91.1 us -> none  [shards(): lax.psum((grad_filters, grad_weight_in, grad_weight_out, grad_gain), 'lat')]
    pallas_call x0 -> x1, Pallas kernels: none -> 49 us  [fused(): pl.pallas_call(functools.partial(fused_kernel, n, rows, lon, scale), out_...]
    psum x1 -> x0, blocking collectives: 30.3 us -> none  [shards(): lax.psum((grad_filters, grad_weight_in, grad_weight_out, grad_gain), 'lat')]
    all_to_all x4 -> x0, waiting for transfers between devices: 21.3 us -> none  [the longest x2 14 us: to_grid(): lax.all_to_all(pieces, 'lat', split_axis=1, concat_axis=3, tiled=True)]
    all_to_all x4 -> x0, starting transfers between devices: 17.9 us -> none  [the longest x2 10.9 us: to_orders(): lax.all_to_all(pieces, 'lat', split_axis=3, concat_axis=1, tiled=True)]
    unnamed x15 -> x28, local copies, waits for them, and re-layouts: 2.82 us -> 14 us
    dot_general x14 -> x0, matrix products: 7.95 us -> none  [the longest x1 1.26 us: shards(): jnp.einsum('bjkc,bjkh->ch', normed, grad_pre, preferred_element_type=jnp....]
    mul x10 -> x0, other arithmetic: 5.03 us -> none  [the longest x1 1.94 us: shards(): grad_weight_in * grad_scale]
  transfers between devices with their start and end apart: 5 -> 0, of which waited for: 5 -> 0; matrix products, arithmetic and copies ran while one was open for 6% -> 0% of each run, Pallas kernels for 0% -> 0%
where the time goes in v1:
time: 64.2 us; the launch traced here: 63.6 us
  Pallas kernels  49 us (76%)
  local copies, waits for them, and re-layouts  14 us (22%)
  between operations  0.66 us (1%)
    pallas_call x1, Pallas kernels, fused(): pl.pallas_call(functools.partial(fused_kernel, n, rows, lon, scale), out_...  49 us
    unnamed x28, local copies, waits for them, and re-layouts  14 us

profile of v1, /device:TPU:0, one launch (start us, length us, event | category | flops | bytes accessed | tf_op | source)
XLA Modules:
  0.0 63.6 jit_solution(5678357497144778712)
XLA Ops:
  0.6 0.0 copy-start
  0.6 1.7 %copy-done = bf16[16,4,3,48,48]{4,3,2,1,0:T(8,128)(2,1)S(1)} copy-done((bf16[16,4,3,48,48]{4,3,2,1,0:T(8,128)(2,1)S(1)}, bf16[16,4,3,48,48]{4,3,2,1,0:T(8,128)(2,1)}, u32[]{:S(2)}) %copy-start) | copy-done | bytes 884760
  2.3 0.0 copy-start.1
  2.3 0.9 %copy-done.1 = bf16[256,512]{1,0:T(8,128)(2,1)S(1)} copy-done((bf16[256,512]{1,0:T(8,128)(2,1)S(1)}, bf16[256,512]{1,0:T(8,128)(2,1)}, u32[]{:S(2)}) %copy-start.1) | copy-done | bytes 262168
  3.3 0.0 copy-start.2
  3.3 0.9 %copy-done.2 = bf16[512,256]{1,0:T(8,128)(2,1)S(1)} copy-done((bf16[512,256]{1,0:T(8,128)(2,1)S(1)}, bf16[512,256]{1,0:T(8,128)(2,1)}, u32[]{:S(2)}) %copy-start.2) | copy-done | bytes 262168
  4.2 0.0 copy-start.3
  4.2 0.9 %copy-done.3 = bf16[1,3,96,256]{3,2,1,0:T(8,128)(2,1)S(1)} copy-done((bf16[1,3,96,256]{3,2,1,0:T(8,128)(2,1)S(1)}, bf16[1,3,96,256]{3,2,1,0:T(8,128)(2,1)}, u32[]{:S(2)}) %copy-start.3) | copy-done | bytes 147480
  5.1 0.0 copy-start.4
  5.1 0.9 %copy-done.4 = bf16[1,3,96,256]{3,2,1,0:T(8,128)(2,1)S(1)} copy-done((bf16[1,3,96,256]{3,2,1,0:T(8,128)(2,1)S(1)}, bf16[1,3,96,256]{3,2,1,0:T(8,128)(2,1)}, u32[]{:S(2)}) %copy-start.4) | copy-done | bytes 147480
  6.0 0.0 copy-start.5
  6.0 0.8 %copy-done.5 = bf16[2,48,256]{2,1,0:T(8,128)(2,1)S(1)} copy-done((bf16[2,48,256]{2,1,0:T(8,128)(2,1)S(1)}, bf16[2,48,256]{2,1,0:T(8,128)(2,1)}, u32[]{:S(2)}) %copy-start.5) | copy-done | bytes 49176
  6.8 0.0 copy-start.6
  6.8 0.8 %copy-done.6 = bf16[128,96]{1,0:T(8,128)(2,1)S(1)} copy-done((bf16[128,96]{1,0:T(8,128)(2,1)S(1)}, bf16[128,96]{1,0:T(8,128)(2,1)}, u32[]{:S(2)}) %copy-start.6) | copy-done | bytes 24600
  7.6 0.0 copy-start.7
  7.6 0.8 %copy-done.7 = bf16[128,96]{1,0:T(8,128)(2,1)S(1)} copy-done((bf16[128,96]{1,0:T(8,128)(2,1)S(1)}, bf16[128,96]{1,0:T(8,128)(2,1)}, u32[]{:S(2)}) %copy-start.7) | copy-done | bytes 24600
  8.3 0.0 copy-start.8
  8.3 0.7 %copy-done.8 = bf16[96,128]{1,0:T(8,128)(2,1)S(1)} copy-done((bf16[96,128]{1,0:T(8,128)(2,1)S(1)}, bf16[96,128]{1,0:T(8,128)(2,1)}, u32[]{:S(2)}) %copy-start.8) | copy-done | bytes 24600
  9.1 0.0 copy-start.9
  9.1 0.7 %copy-done.9 = bf16[96,128]{1,0:T(8,128)(2,1)S(1)} copy-done((bf16[96,128]{1,0:T(8,128)(2,1)S(1)}, bf16[96,128]{1,0:T(8,128)(2,1)}, u32[]{:S(2)}) %copy-start.9) | copy-done | bytes 24600
  9.8 0.0 copy-start.10
  9.8 0.7 %copy-done.10 = f32[256]{0:T(256)S(1)} copy-done((f32[256]{0:T(256)S(1)}, f32[256]{0:T(256)}, u32[]{:S(2)}) %copy-start.10) | copy-done | bytes 1048
  10.5 49.0 %shard_map.154 = (bf16[288,256]{1,0:T(8,128)(2,1)S(1)}, bf16[288,256]{1,0:T(8,128)(2,1)S(1)}, f32[2,48,256]{2,1,0:T(8,128)S(1)}, f32[256,512]{1,0:T(8,128)S(1)},...) custom-call(bf16[288,256]{1,0:T(8,128)(2,1)S(1)} %bitcast.6, bf16[2,48,256]{2,1,0:T(8,128)(2,1)S(1)} %copy-done.5, ...), custom_call_target="tpu_custom_call" | custom-call | tf_op jit(solution)/shard_map/pallas_call | solution.py:616
  59.5 0.7 %copy.23 = bf16[1,3,96,256]{3,2,1,0:T(8,128)(2,1)} copy(bf16[1,3,96,256]{3,2,1,0:T(8,128)(2,1)S(1)} %bitcast.9) | data formatting | bytes 294912
  60.2 0.7 %copy.24 = bf16[1,3,96,256]{3,2,1,0:T(8,128)(2,1)} copy(bf16[1,3,96,256]{3,2,1,0:T(8,128)(2,1)S(1)} %bitcast.8) | data formatting | bytes 294912
  60.8 0.6 %copy.25 = f32[2,48,256]{2,1,0:T(8,128)} copy(f32[2,48,256]{2,1,0:T(8,128)S(1)} %get-tuple-element.26) | data formatting | bytes 196608
  61.5 0.8 %copy.26 = f32[256,512]{1,0:T(8,128)} copy(f32[256,512]{1,0:T(8,128)S(1)} %get-tuple-element.27) | data formatting | bytes 1048576
  62.3 0.8 %copy.27 = f32[512,256]{1,0:T(8,128)} copy(f32[512,256]{1,0:T(8,128)S(1)} %get-tuple-element.28) | data formatting | bytes 1048576
  63.1 0.6 copy.28
Async XLA Ops:
  0.6 1.7 %copy-start = (bf16[16,4,3,48,48]{4,3,2,1,0:T(8,128)(2,1)S(1)}, bf16[16,4,3,48,48]{4,3,2,1,0:T(8,128)(2,1)}, u32[]{:S(2)}) copy-start(bf16[16,4,3,48,48]{4,3,2,1,0:T(8,128)(2,1)} %constant.14.clone.tables) | copy-start | bytes 2654212
  2.3 0.9 %copy-start.1 = (bf16[256,512]{1,0:T(8,128)(2,1)S(1)}, bf16[256,512]{1,0:T(8,128)(2,1)}, u32[]{:S(2)}) copy-start(bf16[256,512]{1,0:T(8,128)(2,1)} %w_in.1) | copy-start | bytes 786436
  3.3 0.9 %copy-start.2 = (bf16[512,256]{1,0:T(8,128)(2,1)S(1)}, bf16[512,256]{1,0:T(8,128)(2,1)}, u32[]{:S(2)}) copy-start(bf16[512,256]{1,0:T(8,128)(2,1)} %w_out.1) | copy-start | bytes 786436
  4.2 0.9 %copy-start.3 = (bf16[1,3,96,256]{3,2,1,0:T(8,128)(2,1)S(1)}, bf16[1,3,96,256]{3,2,1,0:T(8,128)(2,1)}, u32[]{:S(2)}) copy-start(bf16[1,3,96,256]{3,2,1,0:T(8,128)(2,1)} %param.11) | copy-start | bytes 442372
  5.1 0.9 %copy-start.4 = (bf16[1,3,96,256]{3,2,1,0:T(8,128)(2,1)S(1)}, bf16[1,3,96,256]{3,2,1,0:T(8,128)(2,1)}, u32[]{:S(2)}) copy-start(bf16[1,3,96,256]{3,2,1,0:T(8,128)(2,1)} %param.16) | copy-start | bytes 442372
  6.0 0.8 %copy-start.5 = (bf16[2,48,256]{2,1,0:T(8,128)(2,1)S(1)}, bf16[2,48,256]{2,1,0:T(8,128)(2,1)}, u32[]{:S(2)}) copy-start(bf16[2,48,256]{2,1,0:T(8,128)(2,1)} %filters.1) | copy-start | bytes 147460
  6.8 0.8 %copy-start.6 = (bf16[128,96]{1,0:T(8,128)(2,1)S(1)}, bf16[128,96]{1,0:T(8,128)(2,1)}, u32[]{:S(2)}) copy-start(bf16[128,96]{1,0:T(8,128)(2,1)} %constant.12.clone.inv_nk) | copy-start | bytes 73732
  7.6 0.8 %copy-start.7 = (bf16[128,96]{1,0:T(8,128)(2,1)S(1)}, bf16[128,96]{1,0:T(8,128)(2,1)}, u32[]{:S(2)}) copy-start(bf16[128,96]{1,0:T(8,128)(2,1)} %constant.10.clone.fwd_nk) | copy-start | bytes 73732
  8.3 0.7 %copy-start.8 = (bf16[96,128]{1,0:T(8,128)(2,1)S(1)}, bf16[96,128]{1,0:T(8,128)(2,1)}, u32[]{:S(2)}) copy-start(bf16[96,128]{1,0:T(8,128)(2,1)} %constant.13.clone.fwd_kn) | copy-start | bytes 73732
  9.1 0.7 %copy-start.9 = (bf16[96,128]{1,0:T(8,128)(2,1)S(1)}, bf16[96,128]{1,0:T(8,128)(2,1)}, u32[]{:S(2)}) copy-start(bf16[96,128]{1,0:T(8,128)(2,1)} %constant.11.clone.inv_kn) | copy-start | bytes 73732
  9.8 0.7 %copy-start.10 = (f32[256]{0:T(256)S(1)}, f32[256]{0:T(256)}, u32[]{:S(2)}) copy-start(f32[256]{0:T(256)} %param.15) | copy-start | bytes 3076

commit v2 on v1

--- a/solution.py
+++ b/solution.py
@@ -211,6 +211,7 @@
 HALF = 128
 SLOT = 8
 TILE = 16
+VMEM_LIMIT = 62 * 1024 * 1024
 MESH = pl.DeviceIdType.MESH
 
 
@@ -228,12 +229,15 @@
 
 def fused_kernel(
     n, rows, lon, scale,
-    field, filters, w_in, w_out, gain, cot, fwd_nk, inv_kn, inv_nk, fwd_kn, tables,
-    block_out, grad_field, grad_filters, grad_w_in, grad_w_out, grad_gain,
+    field_in, filters_in, w_in_in, w_out_in, gain_in, cot_in, fwd_nk_in, inv_kn_in, inv_nk_in,
+    fwd_kn_in, tables,
+    block_out_to, grad_field_to, grad_filters_to, grad_gain_to, weights_to,
     send, recv, fsend, frecv, fgather, wsend, wpair, wchips, wrecv, wgather,
     table, up, summed, normed, hidden, grad_pre, grad_sum, coeffs,
     x0, x1, y0, y1, f0, f1, nat,
-    send_sem, recv_sem, chip_send, chip_recv, pair_send, pair_recv, table_sem,
+    field, filters, w_in, w_out, gain, cot, fwd_nk, inv_kn, inv_nk, fwd_kn,
+    block_out, grad_field, grad_filters, grad_gain,
+    send_sem, recv_sem, chip_send, chip_recv, pair_send, pair_recv, fetch_sem, store_sem,
 ):
     me = lax.axis_index("lat")
     ens = lax.axis_index("ens")
@@ -252,9 +256,30 @@
         )
         return 0
 
+    fetches = [
+        pltpu.make_async_copy(source, target, fetch_sem.at[i])
+        for i, (source, target) in enumerate(
+            (
+                (field_in, field), (fwd_nk_in, fwd_nk), (cot_in, cot), (w_out_in, w_out),
+                (tables.at[me], table), (filters_in, filters), (inv_kn_in, inv_kn),
+                (w_in_in, w_in), (gain_in, gain), (inv_nk_in, inv_nk), (fwd_kn_in, fwd_kn),
+            )
+        )
+    ]
+    for fetch in fetches:
+        fetch.start()
     lax.fori_loop(1, n, greet, 0)
-    fetch = pltpu.make_async_copy(tables.at[me], table, table_sem)
-    fetch.start()
+
+    stores = [
+        pltpu.make_async_copy(source, target, store_sem.at[i])
+        for i, (source, target) in enumerate(
+            (
+                (block_out, block_out_to), (grad_field, grad_field_to),
+                (grad_filters, grad_filters_to), (grad_gain, grad_gain_to),
+                (wgather, weights_to),
+            )
+        )
+    ]
 
     def exchange(phase, source, target):
         def copy(k):
@@ -331,6 +356,8 @@
                 v[pl.ds(r * rows + m, degrees, stride=SLOT), :] = value[:, at : at + HALF]
 
     start0, arrive0, leave0 = all_to_all(0)
+    for fetch in fetches[:2]:
+        fetch.wait()
     pack_grid(0, [dot(fwd_nk[...], field[pl.ds(j * lon, lon), :]) for j in range(rows)])
     pl.semaphore_wait(barrier, n - 1)
     start0()
@@ -338,10 +365,11 @@
     y1[...] = jnp.zeros_like(y1)
     f0[...] = jnp.zeros_like(f0)
     f1[...] = jnp.zeros_like(f1)
+    for fetch in fetches[2:]:
+        fetch.wait()
     for j in range(rows):
         at = pl.ds(j * lon, lon)
         up[at, :] = dot_nt(cot[at, :], w_out[...])
-    fetch.wait()
     g0 = filters[0].astype(jnp.float32)
     g1 = filters[1].astype(jnp.float32)
     wide = 2 * HALF
@@ -449,6 +477,7 @@
         block_out[at, :] = (
             summed[at, :].astype(jnp.float32) + dot(hidden[at, :], w_out[...])
         ).astype(bf16)
+    stores[0].start()
     pair0.wait_recv()
     scatter_start, scatter_arrive, scatter_leave = chip_exchange(
         0, lambda i: wchips.at[i], lambda i: wrecv.at[i]
@@ -505,6 +534,7 @@
     grad_gain[...] = scale * jnp.concatenate(
         [ftotal[2 * rows : 2 * rows + 1], ftotal[SLOT + 2 * rows : SLOT + 2 * rows + 1]], axis=1
     )
+    stores[3].start()
     fgather[me] = ftotal.astype(bf16)
     start5, arrive5, leave5 = exchange(5, lambda i: fgather.at[me], lambda i: fgather.at[i])
     start5()
@@ -513,6 +543,8 @@
     for j in range(rows):
         at = pl.ds(j * lon, lon)
         grad_field[at, :] = (grad_sum[at, :] + dot(fwd_kn[...], unpack_grid(3, j))).astype(bf16)
+
+    stores[1].start()
 
     gather_arrive()
     pair1 = pair_copy(1, wgather.at[core], wgather.at[core])
@@ -531,8 +563,35 @@
                 ]
             grad_filters[r, :, h * HALF : (h + 1) * HALF] = nat[2 * r + h]
 
+    stores[2].start()
     pair1_in.wait_recv()
-    full = w_in.shape[1]
+    stores[4].start()
+    for leave in (leave0, leave1, leave2, leave3, leave4, leave5, scatter_leave, gather_leave):
+        leave()
+    pair0.wait_send()
+    pair1.wait_send()
+    for store in stores:
+        store.wait()
+
+
+def write_kernel(scale, *refs):
+    count = 5
+    sources, refs = refs[:count], refs[count:]
+    targets, refs = refs[: count + 1], refs[count + 1 :]
+    held, (grad_w_in, grad_w_out, in_sem, out_sem) = refs[:count], refs[count:]
+    wgather = held[-1]
+    loads = [
+        pltpu.make_async_copy(sources[i], held[i], in_sem.at[i]) for i in range(count)
+    ]
+    stores = [
+        pltpu.make_async_copy(source, targets[i], out_sem.at[i])
+        for i, source in enumerate((*held[:-1], grad_w_in, grad_w_out))
+    ]
+    for load in reversed(loads):
+        load.start()
+    loads[-1].wait()
+    _, chips, double, full = wgather.shape
+    mid = double // 2
     for c in (0, 1):
         grad_w_in[pl.ds(c * chips * mid, chips * mid), :] = (
             wgather[c, :, :mid, :].astype(jnp.float32) * scale
@@ -541,11 +600,13 @@
         grad_w_out[pl.ds(2 * c * chips * mid, 2 * chips * mid), :] = jnp.concatenate(
             [both[:, :, : full // 2], both[:, :, full // 2 :]], axis=1
         ).reshape(2 * chips * mid, full // 2)
-
-    for leave in (leave0, leave1, leave2, leave3, leave4, leave5, scatter_leave, gather_leave):
-        leave()
-    pair0.wait_send()
-    pair1.wait_send()
+    stores[-1].start()
+    stores[-2].start()
+    for i in range(count - 1):
+        loads[i].wait()
+        stores[i].start()
+    for store in stores:
+        store.wait()
 
 
 def legendre_constants(total):
@@ -611,7 +672,7 @@
     f32, bf16 = jnp.float32, jnp.bfloat16
     scale = 1.0 / math.sqrt(total * lon)
     constants = fused_constants(n, rows, lon)
-    vmem = pl.BlockSpec(memory_space=pltpu.VMEM)
+    hbm = pl.BlockSpec(memory_space=pltpu.HBM)
     phases = 4
     outs = pl.pallas_call(
         functools.partial(fused_kernel, n, rows, lon, scale),
@@ -619,12 +680,11 @@
             jax.ShapeDtypeStruct((cells, channels), bf16),
             jax.ShapeDtypeStruct((cells, channels), bf16),
             jax.ShapeDtypeStruct((2, total, channels), f32),
-            jax.ShapeDtypeStruct((channels, hid), f32),
-            jax.ShapeDtypeStruct((hid, channels), f32),
             jax.ShapeDtypeStruct((1, channels), f32),
+            jax.ShapeDtypeStruct((2, chips, 2 * mid, hid), bf16),
         ),
-        in_specs=[vmem] * 10 + [pl.BlockSpec(memory_space=pl.ANY)],
-        out_specs=(vmem,) * 6,
+        in_specs=[hbm] * 11,
+        out_specs=(hbm,) * 5,
         scratch_shapes=[
             pltpu.VMEM((phases, n, 2 * rows * SLOT, HALF), bf16),
             pltpu.VMEM((phases, n, 2 * rows * SLOT, HALF), bf16),
@@ -651,25 +711,54 @@
             pltpu.VMEM((n * SLOT, HALF), f32),
             pltpu.VMEM((n * SLOT, HALF), f32),
             pltpu.VMEM((4, total, HALF), f32),
+            pltpu.VMEM((cells, channels), bf16),
+            pltpu.VMEM(filters.shape, bf16),
+            pltpu.VMEM(weight_in.shape, bf16),
+            pltpu.VMEM(weight_out.shape, bf16),
+            pltpu.VMEM((1, channels), f32),
+            pltpu.VMEM((cells, channels), bf16),
+            *[pltpu.VMEM(t.shape, bf16) for t in constants[:4]],
+            pltpu.VMEM((cells, channels), bf16),
+            pltpu.VMEM((cells, channels), bf16),
+            pltpu.VMEM((2, total, channels), f32),
+            pltpu.VMEM((1, channels), f32),
             pltpu.SemaphoreType.DMA((6, n)),
             pltpu.SemaphoreType.DMA((6, n)),
             pltpu.SemaphoreType.DMA((2, chips)),
             pltpu.SemaphoreType.DMA((2, chips)),
             pltpu.SemaphoreType.DMA((2,)),
             pltpu.SemaphoreType.DMA((2,)),
-            pltpu.SemaphoreType.DMA,
+            pltpu.SemaphoreType.DMA((11,)),
+            pltpu.SemaphoreType.DMA((5,)),
         ],
         compiler_params=pltpu.CompilerParams(
-            collective_id=0, has_side_effects=True, vmem_limit_bytes=40 * 1024 * 1024
+            collective_id=0, has_side_effects=True, vmem_limit_bytes=VMEM_LIMIT
         ),
     )(
         field.reshape(cells, channels), filters, weight_in, weight_out,
         norm_gain.reshape(1, channels), cotangent.reshape(cells, channels),
         *[jnp.asarray(t) for t in constants],
     )
+    weight_shapes = ((channels, hid), (hid, channels))
+    outs = pl.pallas_call(
+        functools.partial(write_kernel, scale),
+        out_shape=(
+            *[jax.ShapeDtypeStruct(o.shape, o.dtype) for o in outs[:-1]],
+            *[jax.ShapeDtypeStruct(shape, f32) for shape in weight_shapes],
+        ),
+        in_specs=[hbm] * 5,
+        out_specs=(hbm,) * 6,
+        scratch_shapes=[
+            *[pltpu.VMEM(o.shape, o.dtype) for o in outs],
+            *[pltpu.VMEM(shape, f32) for shape in weight_shapes],
+            pltpu.SemaphoreType.DMA((5,)),
+            pltpu.SemaphoreType.DMA((6,)),
+        ],
+        compiler_params=pltpu.CompilerParams(vmem_limit_bytes=VMEM_LIMIT),
+    )(*outs)
     return (
         outs[0].reshape(field.shape), outs[1].reshape(field.shape),
-        outs[2], outs[3], outs[4], outs[5].reshape(channels),
+        outs[2], outs[4], outs[5], outs[3].reshape(channels),
     )
 
 

time: 64.2 us -> 52.3 us (0.81)
  local copies, waits for them, and re-layouts: 14 us -> 0 us
  Pallas kernels: 49 us -> 51.5 us
    unnamed x28 -> x0, local copies, waits for them, and re-layouts: 14 us -> none
    pallas_call x0 -> x1, Pallas kernels: none -> 2.28 us  [fused(): pl.pallas_call(functools.partial(write_kernel, scale), out_shape=(*[jax.S...]
where the time goes in v2:
time: 52.3 us; the launch traced here: 52.2 us
  Pallas kernels  51.5 us (98%)
  between operations  0.64 us (1%)
    pallas_call x1, Pallas kernels, fused(): pl.pallas_call(functools.partial(fused_kernel, n, rows, lon, scale), out_...  49.3 us
    pallas_call x1, Pallas kernels, fused(): pl.pallas_call(functools.partial(write_kernel, scale), out_shape=(*[jax.S...  2.28 us

profile of v2, /device:TPU:0, one launch (start us, length us, event | category | flops | bytes accessed | tf_op | source)
XLA Modules:
  0.0 52.2 jit_solution(3544297431355518136)
XLA Ops:
  0.6 49.3 %shard_map.154 = (bf16[288,256]{1,0:T(8,128)(2,1)}, bf16[288,256]{1,0:T(8,128)(2,1)}, f32[2,48,256]{2,1,0:T(8,128)}, f32[1,256]{1,0:T(1,128)}, bf16[2,8,32,512]{3,2,1,0:T(8,128)(2,1)}) custom-call(bf16[288,256]{1,0:T(8,128)(2,1)} %bitcast.6, bf16[2,48,256]{2,1,0:T(8,128)(2,1)} %filters_in.1, bf16[256,512]{1,0:T(8,128)(2,1)} %w_in_in.1, ...), custom_call_target="tpu_custom_call" | custom-call | tf_op jit(solution)/shard_map/pallas_call | solution.py:677
  49.9 2.3 %shard_map.155 = (bf16[288,256]{1,0:T(8,128)(2,1)}, bf16[288,256]{1,0:T(8,128)(2,1)}, f32[2,48,256]{2,1,0:T(8,128)}, f32[1,256]{1,0:T(1,128)}, f32[256,512]{1,0:T(8,128)}, /*index=5*/f32[512,256]{1,0:T(8,128)}) custom-call(bf16[288,256]{1,0:T(8,128)(2,1)} %get-tuple-element.17.refs_0_, bf16[288,256]{1,0:T(8,128)(2,1)} %get-tuple-element.18.refs_1_, ...), custom_call_target="tpu_custom_call" | custom-call | tf_op jit(solution)/shard_map/pallas_call | solution.py:743

commit v3 on v2

--- a/solution.py
+++ b/solution.py
@@ -299,7 +299,7 @@
             )
 
         def start(k, _):
-            copy(k).start()
+            copy(n - k).start()
             return 0
 
         def arrive(k, _):
@@ -472,12 +472,6 @@
 
     pair0 = pair_copy(0, wsend.at[1 - core], wpair)
     pair0.start()
-    for j in range(rows):
-        at = pl.ds(j * lon, lon)
-        block_out[at, :] = (
-            summed[at, :].astype(jnp.float32) + dot(hidden[at, :], w_out[...])
-        ).astype(bf16)
-    stores[0].start()
     pair0.wait_recv()
     scatter_start, scatter_arrive, scatter_leave = chip_exchange(
         0, lambda i: wchips.at[i], lambda i: wrecv.at[i]
@@ -528,6 +522,12 @@
     scatter_arrive()
     wgather[core, chip] = jnp.sum(wrecv[...].astype(jnp.float32), axis=0).astype(bf16)
     gather_start()
+    for j in range(rows):
+        at = pl.ds(j * lon, lon)
+        block_out[at, :] = (
+            summed[at, :].astype(jnp.float32) + dot(hidden[at, :], w_out[...])
+        ).astype(bf16)
+    stores[0].start()
 
     arrive4()
     ftotal = jnp.sum(frecv[...].astype(jnp.float32), axis=0)

time: 52.3 us -> 51.7 us (0.989)
  Pallas kernels: 51.5 us -> 50.9 us
    pallas_call x1, Pallas kernels: 49.3 us -> 48.6 us  [fused(): pl.pallas_call(functools.partial(fused_kernel, n, rows, lon, scale), out_...]
where the time goes in v3:
time: 51.7 us; the launch traced here: 51.5 us
  Pallas kernels  50.9 us (98%)
  between operations  0.64 us (1%)
    pallas_call x1, Pallas kernels, fused(): pl.pallas_call(functools.partial(fused_kernel, n, rows, lon, scale), out_...  48.6 us
    pallas_call x1, Pallas kernels, fused(): pl.pallas_call(functools.partial(write_kernel, scale), out_shape=(*[jax.S...  2.28 us

profile of v3, /device:TPU:0, one launch (start us, length us, event | category | flops | bytes accessed | tf_op | source)
XLA Modules:
  0.0 51.5 jit_solution(2613147028819886617)
XLA Ops:
  0.6 48.6 %shard_map.154 = (bf16[288,256]{1,0:T(8,128)(2,1)}, bf16[288,256]{1,0:T(8,128)(2,1)}, f32[2,48,256]{2,1,0:T(8,128)}, f32[1,256]{1,0:T(1,128)}, bf16[2,8,32,512]{3,2,1,0:T(8,128)(2,1)}) custom-call(bf16[288,256]{1,0:T(8,128)(2,1)} %bitcast.6, bf16[2,48,256]{2,1,0:T(8,128)(2,1)} %filters_in.1, bf16[256,512]{1,0:T(8,128)(2,1)} %w_in_in.1, ...), custom_call_target="tpu_custom_call" | custom-call | tf_op jit(solution)/shard_map/pallas_call | solution.py:677
  49.3 2.3 %shard_map.155 = (bf16[288,256]{1,0:T(8,128)(2,1)}, bf16[288,256]{1,0:T(8,128)(2,1)}, f32[2,48,256]{2,1,0:T(8,128)}, f32[1,256]{1,0:T(1,128)}, f32[256,512]{1,0:T(8,128)}, /*index=5*/f32[512,256]{1,0:T(8,128)}) custom-call(bf16[288,256]{1,0:T(8,128)(2,1)} %get-tuple-element.17.refs_0_, bf16[288,256]{1,0:T(8,128)(2,1)} %get-tuple-element.18.refs_1_, ...), custom_call_target="tpu_custom_call" | custom-call | tf_op jit(solution)/shard_map/pallas_call | solution.py:743
